TPU v7x, 32 devices: a whole 2x2x4 slice. The times are simulated.
32 devices in a mesh: grp: 2 (over y), lat: 4 (over z), tm: 2 (over x), chan: 2 (over core).
Axes of the slice: x: 2, y: 2, z: 4, core: 2. Of those that a mesh axis runs over, the one named last changes fastest.
Arguments:
- innovations: bfloat16 [4, 4, 73, 32, 128], P(None, ('grp', 'tm'), None, ('lat', 'chan')), parts along dimension 1, may hold values from -6 to 6
- obs_mask: int32 [4, 8, 4], P(('grp', 'tm'), ('lat', 'chan')), parts along dimension 0, may hold values 0 or 1
- slopes: bfloat16 [4, 128, 32, 128], P(('grp', 'tm'), 'chan', 'lat'), parts along dimension 0, may hold values from -0.14941406 to 1.09375
- layer_of: int32 [2], replicated, may hold values from 0 to 7
- weight_in: bfloat16 [8, 3, 3, 73, 128], P(None, None, None, None, 'chan'), may hold values from -0.1875 to 0.1875
- weight_out: bfloat16 [8, 3, 3, 128, 73], P(None, None, None, 'chan'), may hold values from -0.25 to 0.25
Outputs:
- gradients: float32 [4, 4, 73, 32, 128], P(None, ('grp', 'tm'), None, ('lat', 'chan')), parts along dimension 1
There are 2 independent parts, one for each index of `grp`. A program takes and returns all parts, laid end to end along the dimension named above; an argument that names none is the same for every part. Nothing has to cross between parts.
All inputs are finite; a program needn't handle non-finite values. No bound on the sum of `obs_mask` on one device may be relied on, other than what follows from the above.
Results may differ from a plain program's by a relative error of at most 0.011.
Values may be sent and summed in bfloat16 or wider, within the bound.
A program may use at most 64 MiB of HBM per device.

v0:
```python
import functools

import jax
import jax.numpy as jnp
from jax import lax
from jax.experimental import pallas as pl
from jax.experimental.pallas import tpu as pltpu
from jax.sharding import PartitionSpec as P

MESH = pl.DeviceIdType.MESH
BF16 = jnp.bfloat16
F32 = jnp.float32


def round_up(n, m):
    return -(-n // m) * m


def kernel(dims, layer_ref, mask_ref, inn_hbm, slopes_hbm, w_in_hbm, w_out_hbm, out_ref,
           inn_ref, slopes_ref, w_in_ref, w_out_ref, w_wide, w_tall,
           raw, send_x, adj, slope_f32, slope_rows, slope_win, w1_ref, w2_ref, w1_other,
           w2_other, vs, hs, ss, load_inn, load_rest,
           x_send, x_recv, h_send, h_recv, w_send, w_recv, s_send, s_recv):
    fronts, chans, rows, win, half, band, lats, owners = dims
    pad = send_x.shape[2]
    rims = rows + 4
    hid_rows = rows + 2
    grp = lax.axis_index("grp")
    lat = lax.axis_index("lat")
    tm = lax.axis_index("tm")
    core = lax.axis_index("chan")
    last = owners - 1

    def dev(lat_no, tm_no, core_no):
        return (grp, lat_no, tm_no, core_no)

    barrier = pltpu.get_barrier_semaphore()

    def greet(device):
        pl.semaphore_signal(barrier, inc=1, device_id=device, device_id_type=MESH)

    def inn_copy(f):
        return pltpu.make_async_copy(inn_hbm.at[f], inn_ref.at[f], load_inn.at[f])

    for f in range(fronts):
        inn_copy(f).start()

    lane = lax.broadcasted_iota(jnp.int32, (1, win), 1)
    tiles = mask_ref.shape[0]
    width = win // tiles
    spread = jnp.zeros((1, win), F32)
    for k in range(tiles):
        spread = jnp.where(lane // width == k, mask_ref[k].astype(F32), spread)

    def load_raw(f):
        raw[...] = inn_ref[f].astype(F32).reshape(chans * rows, win)

    def forcing_row(r):
        return raw[pl.ds(r, chans, stride=rows), :] * spread

    def put_out(f, r, value):
        out_ref[pl.ds(f * (chans * rows) + r, chans, stride=rows), :] = value

    starts = (core * 2, (1 - core) * 2)

    def x_copy(k, f):
        return pltpu.make_async_remote_copy(
            src_ref=send_x.at[f, pl.ds(starts[k], 2)], dst_ref=adj.at[f, pl.ds(2 + starts[k], 2)],
            send_sem=x_send.at[k, f], recv_sem=x_recv.at[k, f],
            device_id=dev(lat, lax.rem(tm + owners - 1, owners), core), device_id_type=MESH)

    def put_send(f, r, value):
        send_x[f, r, 0:chans, :] = value.astype(BF16)

    def clear_send():
        if pad > chans:
            for f in range(fronts):
                for r in range(rows):
                    send_x[f, r, chans:pad, :] = jnp.zeros((pad - chans, win), BF16)

    @pl.when(tm == last)
    def _():
        greet(dev(lat, tm - 1, core))
        clear_send()

        for f in range(fronts):
            inn_copy(f).wait()
            load_raw(f)
            for r in range(rows):
                value = forcing_row(r)
                put_out(f, r, value)
                put_send(f, r, value)
            if f == 0:
                pl.semaphore_wait(barrier, 1)
            x_copy(0, f).start()

        for f in range(fronts):
            x_copy(1, f).start()
        for f in range(fronts):
            for k in range(2):
                x_copy(k, f).wait_send()

    @pl.when(tm < last)
    def _():
        has_down = lat > 0
        has_up = lat < lats - 1
        greet(dev(lat, tm + 1, core))
        greet(dev(lat, tm, 1 - core))

        @pl.when(has_down)
        def _():
            greet(dev(lat - 1, tm, 0))
            greet(dev(lat - 1, tm, 1))

        @pl.when(has_up)
        def _():
            greet(dev(lat + 1, tm, 0))
            greet(dev(lat + 1, tm, 1))

        greeted = 2 + 2 * has_down.astype(jnp.int32) + 2 * has_up.astype(jnp.int32)
        if owners > 2:
            @pl.when(tm > 0)
            def _():
                greet(dev(lat, tm - 1, core))
            greeted = greeted + (tm > 0).astype(jnp.int32)
        clear_send()

        loads = [
            pltpu.make_async_copy(slopes_hbm, slopes_ref, load_rest.at[0]),
            pltpu.make_async_copy(w_out_hbm, w_out_ref, load_rest.at[1]),
            pltpu.make_async_copy(w_in_hbm, w_in_ref, load_rest.at[2]),
        ]
        for load in loads:
            load.start()
        w_wide[...] = jnp.zeros_like(w_wide)
        w_tall[...] = jnp.zeros_like(w_tall)

        loads[0].wait()
        slope_f32[...] = slopes_ref[...].astype(F32)
        for r in range(band):
            slope_rows[r] = slope_f32[pl.ds(r, half, stride=band), :].astype(BF16)

        first = (lat == 0) & (core == 0)
        final = (lat == lats - 1) & (core == 1)

        @pl.when(first)
        def _():
            slope_win[:, 0] = jnp.zeros((2, half, win), BF16)
            for f in range(fronts):
                adj[f, 0:2] = jnp.zeros((2, pad, win), BF16)

        @pl.when(final)
        def _():
            slope_win[:, hid_rows - 1] = jnp.zeros((2, half, win), BF16)
            for f in range(fronts):
                adj[f, rims - 2:rims] = jnp.zeros((2, pad, win), BF16)

        layer = layer_ref[tm]
        loads[1].wait()
        for a in range(3):
            for b in range(3):
                w_wide[b, a * half:(a + 1) * half, 0:chans] = w_out_ref[layer, a, b].astype(F32)
        wide = w_wide[0] + pltpu.roll(w_wide[1], pad, 1) + pltpu.roll(w_wide[2], 2 * pad, 1)
        w1_ref[...] = wide.astype(BF16)
        loads[2].wait()
        for a in range(3):
            for b in range(3):
                w_tall[a, b * half:(b + 1) * half, 0:chans] = w_in_ref[layer, a, b].astype(F32)
        for a in range(3):
            w2_ref[a * pad:(a + 1) * pad, :] = w_tall[a].T[0:pad].astype(BF16)

        pl.semaphore_wait(barrier, greeted)

        partner = dev(lat, tm, 1 - core)
        w1_copy = pltpu.make_async_remote_copy(
            src_ref=w1_ref, dst_ref=w1_other, send_sem=w_send.at[0], recv_sem=w_recv.at[0],
            device_id=partner, device_id_type=MESH)
        w2_copy = pltpu.make_async_remote_copy(
            src_ref=w2_ref, dst_ref=w2_other, send_sem=w_send.at[1], recv_sem=w_recv.at[1],
            device_id=partner, device_id_type=MESH)
        own = hid_rows - 1
        mine_from = core * (rows - 1)
        partner_from = (1 - core) * (rows - 1)
        s_copy = pltpu.make_async_remote_copy(
            src_ref=slope_rows.at[pl.ds(partner_from, own)],
            dst_ref=slope_win.at[1, pl.ds(core, own)],
            send_sem=s_send.at[0], recv_sem=s_recv.at[0],
            device_id=partner, device_id_type=MESH)
        s_down = pltpu.make_async_remote_copy(
            src_ref=slope_rows.at[0], dst_ref=slope_win.at[1 - core, hid_rows - 1],
            send_sem=s_send.at[1], recv_sem=s_recv.at[1 + (1 - core)],
            device_id=dev(lat - 1, tm, 1), device_id_type=MESH)
        s_up = pltpu.make_async_remote_copy(
            src_ref=slope_rows.at[band - 1], dst_ref=slope_win.at[core, 0],
            send_sem=s_send.at[2], recv_sem=s_recv.at[1 + core],
            device_id=dev(lat + 1, tm, 0), device_id_type=MESH)

        w1_copy.start()
        s_copy.start()
        w2_copy.start()

        @pl.when(has_down)
        def _():
            s_down.start()

        @pl.when(has_up)
        def _():
            s_up.start()

        slope_win[0, pl.ds(1 - core, own)] = slope_rows[pl.ds(mine_from, own)]

        not_first = jnp.logical_not(first)
        not_final = jnp.logical_not(final)

        def halo_down(f):
            return pltpu.make_async_remote_copy(
                src_ref=adj.at[f, pl.ds(2, 2)], dst_ref=adj.at[f, pl.ds(rims - 2, 2)],
                send_sem=h_send.at[0, f], recv_sem=h_recv.at[0, f],
                device_id=dev(lat - (1 - core), tm, 1 - core), device_id_type=MESH)

        def halo_up(f):
            return pltpu.make_async_remote_copy(
                src_ref=adj.at[f, pl.ds(rows, 2)], dst_ref=adj.at[f, pl.ds(0, 2)],
                send_sem=h_send.at[1, f], recv_sem=h_recv.at[1, f],
                device_id=dev(lat + core, tm, 1 - core), device_id_type=MESH)

        def pass_on(k, f):
            x_copy(k, f).wait_recv()

            @pl.when(not_first & (core == k))
            def _():
                halo_down(f).start()

            @pl.when(not_final & (core == 1 - k))
            def _():
                halo_up(f).start()

        left_edge = lane == 0
        right_edge = lane == win - 1

        def shifts(x):
            ahead = jnp.where(right_edge, 0.0, pltpu.roll(x, win - 1, 1))
            behind = jnp.where(left_edge, 0.0, pltpu.roll(x, 1, 1))
            return ahead.astype(BF16), x.astype(BF16), behind.astype(BF16)

        def spread_rows(f, row_nos):
            for r in row_nos:
                for b, part in enumerate(shifts(adj[f, r].astype(F32))):
                    vs[f % 2, b * pad:(b + 1) * pad, r * win:(r + 1) * win] = part

        def first_conv(f, low, high):
            columns = slice(low * win, high * win)
            for side, w_ref in enumerate((w1_ref, w1_other)):
                hs[f % 2, side, :, columns] = jnp.dot(
                    w_ref[:, 0:3 * pad], vs[f % 2, :, columns], preferred_element_type=F32)

        def compute(f):
            spread_rows(f, (0, 1, rims - 2, rims - 1))
            first_conv(f, 0, 2)
            first_conv(f, rims - 2, rims)
            for side in range(2):
                for p in range(hid_rows):
                    grad = sum(hs[f % 2, side, a * half:(a + 1) * half, (p + 2 - a) * win:(p + 3 - a) * win]
                               for a in range(3))
                    scaled = (slope_win[side, p].astype(F32) * grad).astype(BF16).astype(F32)
                    for b, part in enumerate(shifts(scaled)):
                        ss[f % 2, side, b * half:(b + 1) * half, p * win:(p + 1) * win] = part
            g = (jnp.dot(w2_ref[...], ss[f % 2, 0], preferred_element_type=F32)
                 + jnp.dot(w2_other[...], ss[f % 2, 1], preferred_element_type=F32))
            for r in range(rows):
                total = sum(g[a * pad:(a + 1) * pad, (r + 2 - a) * win:(r + 3 - a) * win]
                            for a in range(3))
                value = adj[f, r + 2].astype(F32) + total + send_x[f, r].astype(F32)
                value = value[0:chans]
                put_out(f, r, value)
                if owners > 2:
                    put_send(f, r, value)

        def finish(pair):
            for f in pair:
                @pl.when(not_final)
                def _():
                    halo_down(f).wait_recv()

                @pl.when(not_first)
                def _():
                    halo_up(f).wait_recv()

            for f in pair:
                compute(f)
            if owners > 2:
                @pl.when(tm > 0)
                def _():
                    for f in pair:
                        for k in range(2):
                            x_copy(k, f).start()

        for f in range(fronts):
            inn_copy(f).wait()
            load_raw(f)
            for r in range(rows):
                put_send(f, r, forcing_row(r))

        def begin(f):
            spread_rows(f, range(2, rows + 2))
            first_conv(f, 2, rows + 2)

        w1_copy.wait_recv()
        w2_copy.wait_recv()
        s_copy.wait_recv()

        @pl.when(has_down & (core == 0))
        def _():
            s_up_recv(slope_win, slope_rows, s_send, s_recv, 0, dev(lat, tm, 1 - core))

        @pl.when(has_up & (core == 1))
        def _():
            s_up_recv(slope_win, slope_rows, s_send, s_recv, hid_rows - 1, dev(lat, tm, 1 - core))

        @pl.loop(0, fronts)
        def _(f):
            pass_on(0, f)

        waiting = []
        for f in range(fronts):
            pass_on(1, f)
            if len(waiting) == 1:
                finish(waiting)
                waiting = []
            begin(f)
            waiting.append(f)
        finish(waiting)

        w1_copy.wait_send()
        w2_copy.wait_send()
        s_copy.wait_send()

        @pl.when(has_down)
        def _():
            s_down.wait_send()

        @pl.when(has_up)
        def _():
            s_up.wait_send()

        @pl.loop(0, fronts)
        def _(f):
            @pl.when(not_first)
            def _():
                halo_down(f).wait_send()

            @pl.when(not_final)
            def _():
                halo_up(f).wait_send()

            if owners > 2:
                @pl.when(tm > 0)
                def _():
                    for k in range(2):
                        x_copy(k, f).wait_send()


def s_up_recv(slope_win, slope_rows, s_send, s_recv, row, device):
    for side in range(2):
        pltpu.make_async_remote_copy(
            src_ref=slope_rows.at[0], dst_ref=slope_win.at[side, row],
            send_sem=s_send.at[1], recv_sem=s_recv.at[1 + side],
            device_id=device, device_id_type=MESH).wait_recv()


def in_hbm(array):
    return pltpu.with_memory_space_constraint(array, pltpu.HBM)


def per_device(mesh, innovations, obs_mask, slopes, layer_of, weight_in, weight_out):
    fronts, secs, chans, rows, win = innovations.shape
    _, half, band, _ = slopes.shape
    owners = mesh.shape["tm"]
    lats = mesh.shape["lat"]
    assert secs == 1 and band == 2 * rows and owners > 1
    pad = round_up(chans, 16)
    rims, hid_rows = rows + 4, rows + 2

    layers = weight_in.shape[0]
    wide = round_up(3 * pad, 128)

    smem = pl.BlockSpec(memory_space=pltpu.SMEM)
    hbm = pl.BlockSpec(memory_space=pltpu.HBM)
    vmem = pl.BlockSpec(memory_space=pltpu.VMEM)
    out = pl.pallas_call(
        functools.partial(kernel, (fronts, chans, rows, win, half, band, lats, owners)),
        out_shape=pltpu.VMEM((fronts * chans * rows, win), F32),
        in_specs=[smem, smem, hbm, hbm, hbm, hbm],
        out_specs=vmem,
        scratch_shapes=[
            pltpu.VMEM((fronts, chans, rows, win), BF16),
            pltpu.VMEM((half * band, win), BF16),
            pltpu.VMEM((layers, 3, 3, half, chans), BF16),
            pltpu.VMEM((layers, 3, 3, half, chans), BF16),
            pltpu.VMEM((3, 3 * half, wide), F32),
            pltpu.VMEM((3, 3 * half, 128), F32),
            pltpu.VMEM((chans * rows, win), F32),
            pltpu.VMEM((fronts, rows, pad, win), BF16),
            pltpu.VMEM((fronts, rims, pad, win), BF16),
            pltpu.VMEM((half * band, win), F32),
            pltpu.VMEM((band, half, win), BF16),
            pltpu.VMEM((2, hid_rows, half, win), BF16),
            pltpu.VMEM((3 * half, wide), BF16),
            pltpu.VMEM((3 * pad, 3 * half), BF16),
            pltpu.VMEM((3 * half, wide), BF16),
            pltpu.VMEM((3 * pad, 3 * half), BF16),
            pltpu.VMEM((2, 3 * pad, rims * win), BF16),
            pltpu.VMEM((2, 2, 3 * half, rims * win), F32),
            pltpu.VMEM((2, 2, 3 * half, hid_rows * win), BF16),
            pltpu.SemaphoreType.DMA((fronts,)),
            pltpu.SemaphoreType.DMA((3,)),
            pltpu.SemaphoreType.DMA((2, fronts)),
            pltpu.SemaphoreType.DMA((2, fronts)),
            pltpu.SemaphoreType.DMA((2, fronts)),
            pltpu.SemaphoreType.DMA((2, fronts)),
            pltpu.SemaphoreType.DMA((2,)),
            pltpu.SemaphoreType.DMA((2,)),
            pltpu.SemaphoreType.DMA((3,)),
            pltpu.SemaphoreType.DMA((3,)),
        ],
        compiler_params=pltpu.CompilerParams(
            collective_id=0, has_side_effects=True, vmem_limit_bytes=32 * 1024 * 1024
        ),
    )(
        in_hbm(layer_of),
        in_hbm(obs_mask.reshape(obs_mask.shape[-1])),
        in_hbm(innovations.reshape(fronts, chans, rows, win)),
        in_hbm(slopes.reshape(half * band, win)),
        in_hbm(weight_in.swapaxes(3, 4)),
        in_hbm(weight_out),
    )
    return out.reshape(innovations.shape)


def solution(mesh):
    return jax.shard_map(
        functools.partial(per_device, mesh),
        mesh=mesh,
        in_specs=(
            P(None, ("grp", "tm"), None, ("lat", "chan"), None),
            P(("grp", "tm"), ("lat", "chan"), None),
            P(("grp", "tm"), "chan", "lat", None),
            P(),
            P(None, None, None, None, "chan"),
            P(None, None, None, "chan", None),
        ),
        out_specs=P(None, ("grp", "tm"), None, ("lat", "chan"), None),
        check_vma=False,
    )
```

profile of v0, /device:TPU:0, one launch (start us, length us, event | category | flops | bytes accessed | tf_op | source)
XLA Modules:
  0.0 16.2 jit_solution(4851931373915078454)
XLA Ops:
  0.0 15.3 %shard_map.64 = f32[1168,128]{1,0:T(8,128)S(1)} custom-call(s32[2]{0:T(128)} %layer_ref.1, s32[4]{0:T(128)} %bitcast.11, bf16[4,73,4,128]{3,2,1,0:T(4,128)(2,1)} %bitcast.9, bf16[512,128]{1,0:T(8,128)(2,1)} %bitcast.10, bf16[8,3,3,64,73]{4,3,2,1,0:T(8,128)(2,1)} %bitcast.8, bf16[8,3,3,64,73]{4,3,2,1,0:T(8,128)(2,1)} %w_out_hbm.1), custom_call_target="tpu_custom_call" | custom-call | tf_op jit(solution)/shard_map/pallas_call | solution.py:390
  15.3 0.8 %copy.9 = f32[4,1,73,4,128]{4,3,2,1,0:T(4,128)} copy(f32[4,1,73,4,128]{4,3,2,1,0:T(4,128)S(1)} %bitcast.7) | data formatting | bytes 1196032
where the time goes:
time: 16.3 us; the launch traced here: 16.2 us
  Pallas kernels  15.3 us (94%)
  local copies, waits for them, and re-layouts  0.82 us (5%)
    pallas_call x1, Pallas kernels, per_device(): pl.pallas_call(functools.partial(kernel, (fronts, chans, rows, win, half,...  15.3 us
    unnamed x1, local copies, waits for them, and re-layouts  0.82 us

commit v1 on v0

--- a/solution.py
+++ b/solution.py
@@ -16,7 +16,391 @@
     return -(-n // m) * m
 
 
-def kernel(dims, layer_ref, mask_ref, inn_hbm, slopes_hbm, w_in_hbm, w_out_hbm, out_ref,
+def pair_kernel(dims, layer_ref, mask_ref, inn_hbm, slopes_hbm, w_in_hbm, w_out_hbm, out_ref,
+                inn_ref, slopes_ref, w_in_ref, w_out_ref, w_wide, w_tall,
+                raw, frc, adj, res, slope_f32, slope_rows, slope_win, w1_ref, w2_ref, w1_other,
+                w2_other, vs, hs, ss, load_inn, load_rest,
+                x_send, x_recv, r_send, r_recv, h_send, h_recv, w_send, w_recv, s_send, s_recv,
+                t_send, t_recv):
+    fronts, chans, rows, win, half, band, lats, owners = dims
+    pad = frc.shape[2]
+    rims = rows + 4
+    hid_rows = rows + 2
+    far = fronts - 1
+    grp = lax.axis_index("grp")
+    lat = lax.axis_index("lat")
+    tm = lax.axis_index("tm")
+    core = lax.axis_index("chan")
+
+    def dev(lat_no, tm_no, core_no):
+        return (grp, lat_no, tm_no, core_no)
+
+    partner = dev(lat, tm, 1 - core)
+    opposite = dev(lat, 1 - tm, core)
+    has_down = lat > 0
+    has_up = lat < lats - 1
+    first = (lat == 0) & (core == 0)
+    final = (lat == lats - 1) & (core == 1)
+    not_first = jnp.logical_not(first)
+    not_final = jnp.logical_not(final)
+
+    barrier = pltpu.get_barrier_semaphore()
+
+    def greet(device):
+        pl.semaphore_signal(barrier, inc=1, device_id=device, device_id_type=MESH)
+
+    greet(opposite)
+
+    @pl.when(has_down)
+    def _():
+        greet(dev(lat - 1, tm, 0))
+        greet(dev(lat - 1, tm, 1))
+
+    @pl.when(has_up)
+    def _():
+        greet(dev(lat + 1, tm, 0))
+        greet(dev(lat + 1, tm, 1))
+
+    greet(partner)
+    greeted = 2 + 2 * has_down.astype(jnp.int32) + 2 * has_up.astype(jnp.int32)
+
+    def inn_copy(f):
+        return pltpu.make_async_copy(inn_hbm.at[f], inn_ref.at[f], load_inn.at[f])
+
+    loads = [
+        pltpu.make_async_copy(slopes_hbm, slopes_ref, load_rest.at[0]),
+        pltpu.make_async_copy(w_out_hbm, w_out_ref, load_rest.at[1]),
+        pltpu.make_async_copy(w_in_hbm, w_in_ref, load_rest.at[2]),
+    ]
+
+    lane = lax.broadcasted_iota(jnp.int32, (1, win), 1)
+    tiles = mask_ref.shape[0]
+    width = win // tiles
+    spread = jnp.zeros((1, win), F32)
+    for k in range(tiles):
+        spread = jnp.where(lane // width == k, mask_ref[k].astype(F32), spread)
+
+    def load_raw(f):
+        raw[...] = inn_ref[f].astype(F32).reshape(chans * rows, win)
+
+    def forcing_row(r):
+        return raw[pl.ds(r, chans, stride=rows), :] * spread
+
+    def put_out(f, r, value):
+        out_ref[pl.ds(f * (chans * rows) + r, chans, stride=rows), :] = value
+
+    starts = (core * 2, (1 - core) * 2)
+
+    def x_copy(k, f):
+        part = adj.at[f, pl.ds(2 + starts[k], 2)]
+        return pltpu.make_async_remote_copy(
+            src_ref=part, dst_ref=part, send_sem=x_send.at[k, f], recv_sem=x_recv.at[k, f],
+            device_id=opposite, device_id_type=MESH)
+
+    def r_copy(k):
+        part = res.at[pl.ds(2 * k, 2)]
+        return pltpu.make_async_remote_copy(
+            src_ref=part, dst_ref=part, send_sem=r_send.at[k], recv_sem=r_recv.at[k],
+            device_id=opposite, device_id_type=MESH)
+
+    spans = ((0, 1), (band - 1, 1), (3 - 2 * core, 4), (1 + 4 * core, 2))
+
+    def t_copy(k):
+        part = slope_rows.at[pl.ds(*spans[k])]
+        return pltpu.make_async_remote_copy(
+            src_ref=part, dst_ref=part, send_sem=t_send.at[k], recv_sem=t_recv.at[k],
+            device_id=opposite, device_id_type=MESH)
+
+    def halo_down(f):
+        return pltpu.make_async_remote_copy(
+            src_ref=adj.at[f, pl.ds(2, 2)], dst_ref=adj.at[f, pl.ds(rims - 2, 2)],
+            send_sem=h_send.at[0, f], recv_sem=h_recv.at[0, f],
+            device_id=dev(lat - (1 - core), tm, 1 - core), device_id_type=MESH)
+
+    def halo_up(f):
+        return pltpu.make_async_remote_copy(
+            src_ref=adj.at[f, pl.ds(rows, 2)], dst_ref=adj.at[f, pl.ds(0, 2)],
+            send_sem=h_send.at[1, f], recv_sem=h_recv.at[1, f],
+            device_id=dev(lat + core, tm, 1 - core), device_id_type=MESH)
+
+    def pass_on(k, f):
+        @pl.when(not_first & (core == k))
+        def _():
+            halo_down(f).start()
+
+        @pl.when(not_final & (core == 1 - k))
+        def _():
+            halo_up(f).start()
+
+    def halos_here(f):
+        @pl.when(not_final)
+        def _():
+            halo_down(f).wait_recv()
+
+        @pl.when(not_first)
+        def _():
+            halo_up(f).wait_recv()
+
+    def halos_sent(f):
+        @pl.when(not_first)
+        def _():
+            halo_down(f).wait_send()
+
+        @pl.when(not_final)
+        def _():
+            halo_up(f).wait_send()
+
+    w1_copy = pltpu.make_async_remote_copy(
+        src_ref=w1_ref, dst_ref=w1_other, send_sem=w_send.at[0], recv_sem=w_recv.at[0],
+        device_id=partner, device_id_type=MESH)
+    w2_copy = pltpu.make_async_remote_copy(
+        src_ref=w2_ref, dst_ref=w2_other, send_sem=w_send.at[1], recv_sem=w_recv.at[1],
+        device_id=partner, device_id_type=MESH)
+    own = hid_rows - 1
+    mine_from = core * (rows - 1)
+    partner_from = (1 - core) * (rows - 1)
+    s_copy = pltpu.make_async_remote_copy(
+        src_ref=slope_rows.at[pl.ds(partner_from, own)],
+        dst_ref=slope_win.at[1, pl.ds(core, own)],
+        send_sem=s_send.at[0], recv_sem=s_recv.at[0],
+        device_id=partner, device_id_type=MESH)
+    s_down = pltpu.make_async_remote_copy(
+        src_ref=slope_rows.at[0], dst_ref=slope_win.at[1 - core, hid_rows - 1],
+        send_sem=s_send.at[1], recv_sem=s_recv.at[1 + (1 - core)],
+        device_id=dev(lat - 1, tm, 1), device_id_type=MESH)
+    s_up = pltpu.make_async_remote_copy(
+        src_ref=slope_rows.at[band - 1], dst_ref=slope_win.at[core, 0],
+        send_sem=s_send.at[2], recv_sem=s_recv.at[1 + core],
+        device_id=dev(lat + 1, tm, 0), device_id_type=MESH)
+
+    def slope_edges_start():
+        @pl.when(has_down)
+        def _():
+            s_down.start()
+
+        @pl.when(has_up)
+        def _():
+            s_up.start()
+
+    def slopes_here():
+        s_copy.wait_recv()
+
+        @pl.when(has_down & (core == 0))
+        def _():
+            s_up_recv(slope_win, slope_rows, s_send, s_recv, 0, partner)
+
+        @pl.when(has_up & (core == 1))
+        def _():
+            s_up_recv(slope_win, slope_rows, s_send, s_recv, hid_rows - 1, partner)
+
+    def own_slopes():
+        slope_win[0, pl.ds(1 - core, own)] = slope_rows[pl.ds(mine_from, own)]
+
+    def all_sent():
+        w1_copy.wait_send()
+        w2_copy.wait_send()
+        s_copy.wait_send()
+
+        @pl.when(has_down)
+        def _():
+            s_down.wait_send()
+
+        @pl.when(has_up)
+        def _():
+            s_up.wait_send()
+
+    def clear_rims():
+        @pl.when(first)
+        def _():
+            slope_win[:, 0] = jnp.zeros((2, half, win), BF16)
+            for f in range(fronts):
+                adj[f, 0:2] = jnp.zeros((2, pad, win), BF16)
+
+        @pl.when(final)
+        def _():
+            slope_win[:, hid_rows - 1] = jnp.zeros((2, half, win), BF16)
+            for f in range(fronts):
+                adj[f, rims - 2:rims] = jnp.zeros((2, pad, win), BF16)
+
+    def prepare_weights():
+        w_wide[...] = jnp.zeros_like(w_wide)
+        w_tall[...] = jnp.zeros_like(w_tall)
+        layer = layer_ref[0]
+        loads[1].wait()
+        for a in range(3):
+            for b in range(3):
+                w_wide[b, a * half:(a + 1) * half, 0:chans] = w_out_ref[layer, a, b].astype(F32)
+        wide = w_wide[0] + pltpu.roll(w_wide[1], pad, 1) + pltpu.roll(w_wide[2], 2 * pad, 1)
+        w1_ref[...] = wide.astype(BF16)
+        loads[2].wait()
+        for a in range(3):
+            for b in range(3):
+                w_tall[a, b * half:(b + 1) * half, 0:chans] = w_in_ref[layer, a, b].astype(F32)
+        for a in range(3):
+            w2_ref[a * pad:(a + 1) * pad, :] = w_tall[a].T[0:pad].astype(BF16)
+
+    left_edge = lane == 0
+    right_edge = lane == win - 1
+
+    def shifts(x):
+        ahead = jnp.where(right_edge, 0.0, pltpu.roll(x, win - 1, 1))
+        behind = jnp.where(left_edge, 0.0, pltpu.roll(x, 1, 1))
+        return ahead.astype(BF16), x.astype(BF16), behind.astype(BF16)
+
+    def spread_rows(f, row_nos):
+        for r in row_nos:
+            for b, part in enumerate(shifts(adj[f, r].astype(F32))):
+                vs[f % 2, b * pad:(b + 1) * pad, r * win:(r + 1) * win] = part
+
+    def first_conv(f, low, high):
+        columns = slice(low * win, high * win)
+        for side, w_ref in enumerate((w1_ref, w1_other)):
+            hs[f % 2, side, :, columns] = jnp.dot(
+                w_ref[:, 0:3 * pad], vs[f % 2, :, columns], preferred_element_type=F32)
+
+    def begin(f):
+        spread_rows(f, range(2, rows + 2))
+        first_conv(f, 2, rows + 2)
+
+    def rim_conv(f):
+        spread_rows(f, (0, 1, rims - 2, rims - 1))
+        first_conv(f, 0, 2)
+        first_conv(f, rims - 2, rims)
+
+    def rest(f):
+        for side in range(2):
+            for p in range(hid_rows):
+                grad = sum(hs[f % 2, side, a * half:(a + 1) * half, (p + 2 - a) * win:(p + 3 - a) * win]
+                           for a in range(3))
+                scaled = (slope_win[side, p].astype(F32) * grad).astype(BF16).astype(F32)
+                for b, part in enumerate(shifts(scaled)):
+                    ss[f % 2, side, b * half:(b + 1) * half, p * win:(p + 1) * win] = part
+        g = (jnp.dot(w2_ref[...], ss[f % 2, 0], preferred_element_type=F32)
+             + jnp.dot(w2_other[...], ss[f % 2, 1], preferred_element_type=F32))
+        return [adj[f, r + 2].astype(F32)
+                + sum(g[a * pad:(a + 1) * pad, (r + 2 - a) * win:(r + 3 - a) * win] for a in range(3))
+                for r in range(rows)]
+
+    @pl.when(tm == 1)
+    def _():
+        for f in range(fronts):
+            inn_copy(f).start()
+        for load in loads[1:]:
+            load.start()
+        clear_rims()
+        if pad > chans:
+            for f in range(fronts):
+                for r in range(rows):
+                    adj[f, r + 2, chans:pad, :] = jnp.zeros((pad - chans, win), BF16)
+
+        for f in range(fronts):
+            inn_copy(f).wait()
+            load_raw(f)
+            for r in range(rows):
+                value = forcing_row(r)
+                adj[f, r + 2, 0:chans, :] = value.astype(BF16)
+                put_out(f, r, value)
+        pl.semaphore_wait(barrier, greeted)
+        for f in range(far):
+            x_copy(0, f).start()
+        for f in range(far):
+            x_copy(1, f).start()
+        pass_on(0, far)
+        pass_on(1, far)
+        prepare_weights()
+        w1_copy.start()
+        w2_copy.start()
+
+        t_copy(0).wait_recv()
+        t_copy(1).wait_recv()
+        slope_edges_start()
+        w1_copy.wait_recv()
+        begin(far)
+        halos_here(far)
+        rim_conv(far)
+        w2_copy.wait_recv()
+        t_copy(2).wait_recv()
+        s_copy.start()
+        t_copy(3).wait_recv()
+        own_slopes()
+        slopes_here()
+        for r, value in enumerate(rest(far)):
+            res[r] = value.astype(BF16)
+            if r % 2 == 1:
+                r_copy(r // 2).start()
+
+        all_sent()
+        halos_sent(far)
+        for k in range(2):
+            for f in range(far):
+                x_copy(k, f).wait_send()
+        for k in range(2):
+            r_copy(k).wait_send()
+
+    @pl.when(tm == 0)
+    def _():
+        for load in loads:
+            load.start()
+        for f in range(fronts):
+            inn_copy(f).start()
+        clear_rims()
+
+        loads[0].wait()
+        slope_f32[...] = slopes_ref[...].astype(F32)
+        for r in range(band):
+            slope_rows[r] = slope_f32[pl.ds(r, half, stride=band), :].astype(BF16)
+        own_slopes()
+        prepare_weights()
+
+        pl.semaphore_wait(barrier, greeted)
+        for k in range(4):
+            t_copy(k).start()
+        slope_edges_start()
+        w1_copy.start()
+        s_copy.start()
+        w2_copy.start()
+
+        for f in range(fronts):
+            inn_copy(f).wait()
+            load_raw(f)
+            for r in range(rows):
+                frc[f, r, 0:chans, :] = forcing_row(r).astype(BF16)
+
+        for f in range(far):
+            x_copy(0, f).wait_recv()
+            pass_on(0, f)
+
+        w1_copy.wait_recv()
+        w2_copy.wait_recv()
+        slopes_here()
+
+        def finish(f):
+            halos_here(f)
+            rim_conv(f)
+            for r, value in enumerate(rest(f)):
+                put_out(f, r, value[0:chans] + frc[f, r, 0:chans, :].astype(F32))
+
+        for f in range(far):
+            x_copy(1, f).wait_recv()
+            pass_on(1, f)
+            if f > 0:
+                finish(f - 1)
+            begin(f)
+        finish(far - 1)
+
+        for k in range(2):
+            r_copy(k).wait_recv()
+            for r in (2 * k, 2 * k + 1):
+                put_out(far, r, res[r, 0:chans, :].astype(F32) + frc[far, r, 0:chans, :].astype(F32))
+
+        all_sent()
+        for f in range(far):
+            halos_sent(f)
+        for k in range(4):
+            t_copy(k).wait_send()
+
+
+def chain_kernel(dims, layer_ref, mask_ref, inn_hbm, slopes_hbm, w_in_hbm, w_out_hbm, out_ref,
            inn_ref, slopes_ref, w_in_ref, w_out_ref, w_wide, w_tall,
            raw, send_x, adj, slope_f32, slope_rows, slope_win, w1_ref, w2_ref, w1_other,
            w2_other, vs, hs, ss, load_inn, load_rest,
@@ -377,7 +761,8 @@
     _, half, band, _ = slopes.shape
     owners = mesh.shape["tm"]
     lats = mesh.shape["lat"]
-    assert secs == 1 and band == 2 * rows and owners > 1
+    assert secs == 1 and band == 2 * rows and rows == 4 and owners > 1
+    pair = owners == 2 and fronts > 1
     pad = round_up(chans, 16)
     rims, hid_rows = rows + 4, rows + 2
 
@@ -388,7 +773,7 @@
     hbm = pl.BlockSpec(memory_space=pltpu.HBM)
     vmem = pl.BlockSpec(memory_space=pltpu.VMEM)
     out = pl.pallas_call(
-        functools.partial(kernel, (fronts, chans, rows, win, half, band, lats, owners)),
+        functools.partial(pair_kernel if pair else chain_kernel, (fronts, chans, rows, win, half, band, lats, owners)),
         out_shape=pltpu.VMEM((fronts * chans * rows, win), F32),
         in_specs=[smem, smem, hbm, hbm, hbm, hbm],
         out_specs=vmem,
@@ -402,6 +787,7 @@
             pltpu.VMEM((chans * rows, win), F32),
             pltpu.VMEM((fronts, rows, pad, win), BF16),
             pltpu.VMEM((fronts, rims, pad, win), BF16),
+            *([pltpu.VMEM((rows, pad, win), BF16)] if pair else []),
             pltpu.VMEM((half * band, win), F32),
             pltpu.VMEM((band, half, win), BF16),
             pltpu.VMEM((2, hid_rows, half, win), BF16),
@@ -416,12 +802,14 @@
             pltpu.SemaphoreType.DMA((3,)),
             pltpu.SemaphoreType.DMA((2, fronts)),
             pltpu.SemaphoreType.DMA((2, fronts)),
+            *([pltpu.SemaphoreType.DMA((2,))] * 2 if pair else []),
             pltpu.SemaphoreType.DMA((2, fronts)),
             pltpu.SemaphoreType.DMA((2, fronts)),
             pltpu.SemaphoreType.DMA((2,)),
             pltpu.SemaphoreType.DMA((2,)),
             pltpu.SemaphoreType.DMA((3,)),
             pltpu.SemaphoreType.DMA((3,)),
+            *([pltpu.SemaphoreType.DMA((4,))] * 2 if pair else []),
         ],
         compiler_params=pltpu.CompilerParams(
             collective_id=0, has_side_effects=True, vmem_limit_bytes=32 * 1024 * 1024

time: 16.3 us -> 15.4 us (0.945)
  Pallas kernels: 15.3 us -> 14.4 us
    pallas_call x1, Pallas kernels: 15.3 us -> 14.4 us  [per_device(): pl.pallas_call(functools.partial(pair_kernel if pair else chain_kernel, (...]
where the time goes in v1:
time: 15.4 us; the launch traced here: 15.2 us
  Pallas kernels  14.4 us (94%)
  local copies, waits for them, and re-layouts  0.82 us (5%)
    pallas_call x1, Pallas kernels, per_device(): pl.pallas_call(functools.partial(pair_kernel if pair else chain_kernel, (...  14.4 us
    unnamed x1, local copies, waits for them, and re-layouts  0.82 us

profile of v1, /device:TPU:0, one launch (start us, length us, event | category | flops | bytes accessed | tf_op | source)
XLA Modules:
  0.0 15.2 jit_solution(15284806514071417755)
XLA Ops:
  0.0 14.4 %shard_map.64 = f32[1168,128]{1,0:T(8,128)S(1)} custom-call(s32[2]{0:T(128)} %layer_ref.1, s32[4]{0:T(128)} %bitcast.11, bf16[4,73,4,128]{3,2,1,0:T(4,128)(2,1)} %bitcast.9, bf16[512,128]{1,0:T(8,128)(2,1)} %bitcast.10, bf16[8,3,3,64,73]{4,3,2,1,0:T(8,128)(2,1)} %bitcast.8, bf16[8,3,3,64,73]{4,3,2,1,0:T(8,128)(2,1)} %w_out_hbm.1), custom_call_target="tpu_custom_call" | custom-call | tf_op jit(solution)/shard_map/pallas_call | solution.py:775
  14.4 0.8 %copy.9 = f32[4,1,73,4,128]{4,3,2,1,0:T(4,128)} copy(f32[4,1,73,4,128]{4,3,2,1,0:T(4,128)S(1)} %bitcast.7) | data formatting | bytes 1196032

commit v2 on v1

--- a/solution.py
+++ b/solution.py
@@ -21,7 +21,7 @@
                 raw, frc, adj, res, slope_f32, slope_rows, slope_win, w1_ref, w2_ref, w1_other,
                 w2_other, vs, hs, ss, load_inn, load_rest,
                 x_send, x_recv, r_send, r_recv, h_send, h_recv, w_send, w_recv, s_send, s_recv,
-                t_send, t_recv):
+                t_send, t_recv, above):
     fronts, chans, rows, win, half, band, lats, owners = dims
     pad = frc.shape[2]
     rims = rows + 4
@@ -51,18 +51,43 @@
 
     greet(opposite)
 
-    @pl.when(has_down)
-    def _():
-        greet(dev(lat - 1, tm, 0))
-        greet(dev(lat - 1, tm, 1))
-
     @pl.when(has_up)
     def _():
         greet(dev(lat + 1, tm, 0))
-        greet(dev(lat + 1, tm, 1))
+
+        @pl.when(core == 1)
+        def _():
+            greet(dev(lat + 1, tm, 1))
+
+        @pl.when(tm == 0)
+        def _():
+            greet(dev(lat + 1, 1, 0))
+
+        @pl.when((tm == 1) & (core == 1))
+        def _():
+            greet(dev(lat + 1, 0, 0))
+            greet(dev(lat + 1, 0, 1))
 
     greet(partner)
-    greeted = 2 + 2 * has_down.astype(jnp.int32) + 2 * has_up.astype(jnp.int32)
+    below = has_down.astype(jnp.int32)
+
+    def enter():
+        pl.semaphore_wait(barrier, 2 + below * (2 - core + (1 - tm) + 2 * tm * (1 - core)))
+
+        @pl.when(has_down & (core == 0))
+        def _():
+            for c in range(2):
+                pl.semaphore_signal(above, inc=1, device_id=dev(lat - 1, tm, c), device_id_type=MESH)
+
+        @pl.when(has_down & (core == 0) & (tm == 1))
+        def _():
+            for c in range(2):
+                pl.semaphore_signal(above, inc=1, device_id=dev(lat - 1, 0, c), device_id_type=MESH)
+
+    def wait_above():
+        @pl.when(has_up)
+        def _():
+            pl.semaphore_wait(above, 2 - tm)
 
     def inn_copy(f):
         return pltpu.make_async_copy(inn_hbm.at[f], inn_ref.at[f], load_inn.at[f])
@@ -103,7 +128,7 @@
             src_ref=part, dst_ref=part, send_sem=r_send.at[k], recv_sem=r_recv.at[k],
             device_id=opposite, device_id_type=MESH)
 
-    spans = ((0, 1), (band - 1, 1), (3 - 2 * core, 4), (1 + 4 * core, 2))
+    spans = ((3 - 3 * core, 5), (5 * core, 3))
 
     def t_copy(k):
         part = slope_rows.at[pl.ds(*spans[k])]
@@ -164,23 +189,31 @@
         dst_ref=slope_win.at[1, pl.ds(core, own)],
         send_sem=s_send.at[0], recv_sem=s_recv.at[0],
         device_id=partner, device_id_type=MESH)
-    s_down = pltpu.make_async_remote_copy(
-        src_ref=slope_rows.at[0], dst_ref=slope_win.at[1 - core, hid_rows - 1],
-        send_sem=s_send.at[1], recv_sem=s_recv.at[1 + (1 - core)],
-        device_id=dev(lat - 1, tm, 1), device_id_type=MESH)
-    s_up = pltpu.make_async_remote_copy(
-        src_ref=slope_rows.at[band - 1], dst_ref=slope_win.at[core, 0],
-        send_sem=s_send.at[2], recv_sem=s_recv.at[1 + core],
-        device_id=dev(lat + 1, tm, 0), device_id_type=MESH)
-
-    def slope_edges_start():
+
+    def s_down(to, k):
+        return pltpu.make_async_remote_copy(
+            src_ref=slope_rows.at[0], dst_ref=slope_win.at[1 - core, hid_rows - 1],
+            send_sem=s_send.at[1 + k], recv_sem=s_recv.at[1 + (1 - core)],
+            device_id=dev(lat - 1, to, 1), device_id_type=MESH)
+
+    def s_up(to, k):
+        return pltpu.make_async_remote_copy(
+            src_ref=slope_rows.at[band - 1], dst_ref=slope_win.at[core, 0],
+            send_sem=s_send.at[3 + k], recv_sem=s_recv.at[1 + core],
+            device_id=dev(lat + 1, to, 0), device_id_type=MESH)
+
+    def slope_down(act, to):
         @pl.when(has_down)
         def _():
-            s_down.start()
-
+            act(s_down(to, to))
+
+    def slope_up(act, to):
         @pl.when(has_up)
         def _():
-            s_up.start()
+            act(s_up(to, to))
+
+    def start(copy):
+        copy.start()
 
     def slopes_here():
         s_copy.wait_recv()
@@ -200,14 +233,6 @@
         w1_copy.wait_send()
         w2_copy.wait_send()
         s_copy.wait_send()
-
-        @pl.when(has_down)
-        def _():
-            s_down.wait_send()
-
-        @pl.when(has_up)
-        def _():
-            s_up.wait_send()
 
     def clear_rims():
         @pl.when(first)
@@ -293,35 +318,39 @@
                 for r in range(rows):
                     adj[f, r + 2, chans:pad, :] = jnp.zeros((pad - chans, win), BF16)
 
-        for f in range(fronts):
+        def take(f):
             inn_copy(f).wait()
             load_raw(f)
             for r in range(rows):
-                value = forcing_row(r)
-                adj[f, r + 2, 0:chans, :] = value.astype(BF16)
-                put_out(f, r, value)
-        pl.semaphore_wait(barrier, greeted)
-        for f in range(far):
+                adj[f, r + 2, 0:chans, :] = forcing_row(r).astype(BF16)
+
+        take(0)
+        enter()
+        x_copy(0, 0).start()
+        for f in range(1, far):
+            take(f)
             x_copy(0, f).start()
         for f in range(far):
             x_copy(1, f).start()
+        take(far)
+        wait_above()
         pass_on(0, far)
         pass_on(1, far)
         prepare_weights()
         w1_copy.start()
         w2_copy.start()
-
-        t_copy(0).wait_recv()
-        t_copy(1).wait_recv()
-        slope_edges_start()
+        for f in range(fronts):
+            for r in range(rows):
+                put_out(f, r, adj[f, r + 2, 0:chans, :].astype(F32))
+
         w1_copy.wait_recv()
         begin(far)
         halos_here(far)
         rim_conv(far)
         w2_copy.wait_recv()
-        t_copy(2).wait_recv()
+        t_copy(0).wait_recv()
         s_copy.start()
-        t_copy(3).wait_recv()
+        t_copy(1).wait_recv()
         own_slopes()
         slopes_here()
         for r, value in enumerate(rest(far)):
@@ -349,15 +378,18 @@
         slope_f32[...] = slopes_ref[...].astype(F32)
         for r in range(band):
             slope_rows[r] = slope_f32[pl.ds(r, half, stride=band), :].astype(BF16)
+        enter()
+        slope_down(start, 1)
+        for k in range(2):
+            t_copy(k).start()
+        slope_down(start, 0)
+        s_copy.start()
         own_slopes()
         prepare_weights()
-
-        pl.semaphore_wait(barrier, greeted)
-        for k in range(4):
-            t_copy(k).start()
-        slope_edges_start()
+        wait_above()
+        slope_up(start, 1)
+        slope_up(start, 0)
         w1_copy.start()
-        s_copy.start()
         w2_copy.start()
 
         for f in range(fronts):
@@ -396,8 +428,10 @@
         all_sent()
         for f in range(far):
             halos_sent(f)
-        for k in range(4):
+        for k in range(2):
             t_copy(k).wait_send()
+            slope_down(lambda copy: copy.wait_send(), k)
+            slope_up(lambda copy: copy.wait_send(), k)
 
 
 def chain_kernel(dims, layer_ref, mask_ref, inn_hbm, slopes_hbm, w_in_hbm, w_out_hbm, out_ref,
@@ -807,9 +841,9 @@
             pltpu.SemaphoreType.DMA((2, fronts)),
             pltpu.SemaphoreType.DMA((2,)),
             pltpu.SemaphoreType.DMA((2,)),
+            pltpu.SemaphoreType.DMA((5,)),
             pltpu.SemaphoreType.DMA((3,)),
-            pltpu.SemaphoreType.DMA((3,)),
-            *([pltpu.SemaphoreType.DMA((4,))] * 2 if pair else []),
+            *([pltpu.SemaphoreType.DMA((2,))] * 2 + [pltpu.SemaphoreType.REGULAR] if pair else []),
         ],
         compiler_params=pltpu.CompilerParams(
             collective_id=0, has_side_effects=True, vmem_limit_bytes=32 * 1024 * 1024

time: 15.4 us -> 15.1 us (0.981)
  Pallas kernels: 14.4 us -> 14.1 us
    pallas_call x1, Pallas kernels: 14.4 us -> 14.1 us  [per_device(): pl.pallas_call(functools.partial(pair_kernel if pair else chain_kernel, (...]
where the time goes in v2:
time: 15.1 us; the launch traced here: 14.9 us
  Pallas kernels  14.1 us (93%)
  local copies, waits for them, and re-layouts  0.82 us (5%)
    pallas_call x1, Pallas kernels, per_device(): pl.pallas_call(functools.partial(pair_kernel if pair else chain_kernel, (...  14.1 us
    unnamed x1, local copies, waits for them, and re-layouts  0.82 us

profile of v2, /device:TPU:0, one launch (start us, length us, event | category | flops | bytes accessed | tf_op | source)
XLA Modules:
  0.0 14.9 jit_solution(14704096212679541720)
XLA Ops:
  0.0 14.1 %shard_map.64 = f32[1168,128]{1,0:T(8,128)S(1)} custom-call(s32[2]{0:T(128)} %layer_ref.1, s32[4]{0:T(128)} %bitcast.11, bf16[4,73,4,128]{3,2,1,0:T(4,128)(2,1)} %bitcast.9, bf16[512,128]{1,0:T(8,128)(2,1)} %bitcast.10, bf16[8,3,3,64,73]{4,3,2,1,0:T(8,128)(2,1)} %bitcast.8, bf16[8,3,3,64,73]{4,3,2,1,0:T(8,128)(2,1)} %w_out_hbm.1), custom_call_target="tpu_custom_call" | custom-call | tf_op jit(solution)/shard_map/pallas_call | solution.py:809
  14.1 0.8 %copy.9 = f32[4,1,73,4,128]{4,3,2,1,0:T(4,128)} copy(f32[4,1,73,4,128]{4,3,2,1,0:T(4,128)S(1)} %bitcast.7) | data formatting | bytes 1196032

commit v3 on v2

--- a/solution.py
+++ b/solution.py
@@ -327,29 +327,46 @@
         take(0)
         enter()
         x_copy(0, 0).start()
+
+        @pl.when(core == 1)
+        def _():
+            x_copy(0, 0).wait_send()
+
         for f in range(1, far):
             take(f)
             x_copy(0, f).start()
         for f in range(far):
             x_copy(1, f).start()
         take(far)
-        wait_above()
-        pass_on(0, far)
-        pass_on(1, far)
+
+        @pl.when(not_first)
+        def _():
+            halo_down(far).start()
+
+        @pl.when(not_final & (core == 0))
+        def _():
+            halo_up(far).start()
+
         prepare_weights()
         w1_copy.start()
         w2_copy.start()
+        wait_above()
+
+        @pl.when(not_final & (core == 1))
+        def _():
+            halo_up(far).start()
+
         for f in range(fronts):
             for r in range(rows):
                 put_out(f, r, adj[f, r + 2, 0:chans, :].astype(F32))
 
         w1_copy.wait_recv()
         begin(far)
+        t_copy(0).wait_recv()
+        s_copy.start()
         halos_here(far)
         rim_conv(far)
         w2_copy.wait_recv()
-        t_copy(0).wait_recv()
-        s_copy.start()
         t_copy(1).wait_recv()
         own_slopes()
         slopes_here()
@@ -360,8 +377,12 @@
 
         all_sent()
         halos_sent(far)
+        @pl.when(core == 0)
+        def _():
+            x_copy(0, 0).wait_send()
+
         for k in range(2):
-            for f in range(far):
+            for f in range(1 - k, far):
                 x_copy(k, f).wait_send()
         for k in range(2):
             r_copy(k).wait_send()

time: 15.1 us -> 14.5 us (0.960)
  Pallas kernels: 14.1 us -> 13.5 us
    pallas_call x1, Pallas kernels: 14.1 us -> 13.5 us  [per_device(): pl.pallas_call(functools.partial(pair_kernel if pair else chain_kernel, (...]
where the time goes in v3:
time: 14.5 us; the launch traced here: 14.4 us
  Pallas kernels  13.5 us (93%)
  local copies, waits for them, and re-layouts  0.82 us (6%)
    pallas_call x1, Pallas kernels, per_device(): pl.pallas_call(functools.partial(pair_kernel if pair else chain_kernel, (...  13.5 us
    unnamed x1, local copies, waits for them, and re-layouts  0.82 us

profile of v3, /device:TPU:0, one launch (start us, length us, event | category | flops | bytes accessed | tf_op | source)
XLA Modules:
  0.0 14.4 jit_solution(461659562311670021)
XLA Ops:
  0.0 13.5 %shard_map.64 = f32[1168,128]{1,0:T(8,128)S(1)} custom-call(s32[2]{0:T(128)} %layer_ref.1, s32[4]{0:T(128)} %bitcast.11, bf16[4,73,4,128]{3,2,1,0:T(4,128)(2,1)} %bitcast.9, bf16[512,128]{1,0:T(8,128)(2,1)} %bitcast.10, bf16[8,3,3,64,73]{4,3,2,1,0:T(8,128)(2,1)} %bitcast.8, bf16[8,3,3,64,73]{4,3,2,1,0:T(8,128)(2,1)} %w_out_hbm.1), custom_call_target="tpu_custom_call" | custom-call | tf_op jit(solution)/shard_map/pallas_call | solution.py:830
  13.5 0.8 %copy.9 = f32[4,1,73,4,128]{4,3,2,1,0:T(4,128)} copy(f32[4,1,73,4,128]{4,3,2,1,0:T(4,128)S(1)} %bitcast.7) | data formatting | bytes 1196032

commit v4 on v3

--- a/solution.py
+++ b/solution.py
@@ -18,8 +18,7 @@
 
 def pair_kernel(dims, layer_ref, mask_ref, inn_hbm, slopes_hbm, w_in_hbm, w_out_hbm, out_ref,
                 inn_ref, slopes_ref, w_in_ref, w_out_ref, w_wide, w_tall,
-                raw, frc, adj, res, slope_f32, slope_rows, slope_win, w1_ref, w2_ref, w1_other,
-                w2_other, vs, hs, ss, load_inn, load_rest,
+                raw, frc, adj, res, slope_f32, slope_rows, slope_win, w1_ref, w2_ref, vs, hs, ss, load_inn, load_rest,
                 x_send, x_recv, r_send, r_recv, h_send, h_recv, w_send, w_recv, s_send, s_recv,
                 t_send, t_recv, above):
     fronts, chans, rows, win, half, band, lats, owners = dims
@@ -27,6 +26,7 @@
     rims = rows + 4
     hid_rows = rows + 2
     far = fronts - 1
+    deep = w2_ref.shape[1] // 2
     grp = lax.axis_index("grp")
     lat = lax.axis_index("lat")
     tm = lax.axis_index("tm")
@@ -176,10 +176,11 @@
             halo_up(f).wait_send()
 
     w1_copy = pltpu.make_async_remote_copy(
-        src_ref=w1_ref, dst_ref=w1_other, send_sem=w_send.at[0], recv_sem=w_recv.at[0],
+        src_ref=w1_ref.at[0], dst_ref=w1_ref.at[1], send_sem=w_send.at[0], recv_sem=w_recv.at[0],
         device_id=partner, device_id_type=MESH)
     w2_copy = pltpu.make_async_remote_copy(
-        src_ref=w2_ref, dst_ref=w2_other, send_sem=w_send.at[1], recv_sem=w_recv.at[1],
+        src_ref=w2_ref.at[:, pl.ds(0, deep)], dst_ref=w2_ref.at[:, pl.ds(deep, deep)],
+        send_sem=w_send.at[1], recv_sem=w_recv.at[1],
         device_id=partner, device_id_type=MESH)
     own = hid_rows - 1
     mine_from = core * (rows - 1)
@@ -250,19 +251,24 @@
     def prepare_weights():
         w_wide[...] = jnp.zeros_like(w_wide)
         w_tall[...] = jnp.zeros_like(w_tall)
+        if deep > 3 * half:
+            w2_ref[:, 3 * half:deep] = jnp.zeros((3 * pad, deep - 3 * half), BF16)
+            for side in range(2):
+                ss[:, side * deep + 3 * half:(side + 1) * deep] = jnp.zeros(
+                    (2, deep - 3 * half, hid_rows * win), BF16)
         layer = layer_ref[0]
         loads[1].wait()
         for a in range(3):
             for b in range(3):
                 w_wide[b, a * half:(a + 1) * half, 0:chans] = w_out_ref[layer, a, b].astype(F32)
         wide = w_wide[0] + pltpu.roll(w_wide[1], pad, 1) + pltpu.roll(w_wide[2], 2 * pad, 1)
-        w1_ref[...] = wide.astype(BF16)
+        w1_ref[0] = wide.astype(BF16)
         loads[2].wait()
         for a in range(3):
             for b in range(3):
                 w_tall[a, b * half:(b + 1) * half, 0:chans] = w_in_ref[layer, a, b].astype(F32)
         for a in range(3):
-            w2_ref[a * pad:(a + 1) * pad, :] = w_tall[a].T[0:pad].astype(BF16)
+            w2_ref[a * pad:(a + 1) * pad, 0:3 * half] = w_tall[a].T[0:pad].astype(BF16)
 
     left_edge = lane == 0
     right_edge = lane == win - 1
@@ -272,39 +278,50 @@
         behind = jnp.where(left_edge, 0.0, pltpu.roll(x, 1, 1))
         return ahead.astype(BF16), x.astype(BF16), behind.astype(BF16)
 
+    place = [*range(rows, rows + 2), *range(rows), *range(rows + 2, rims)]
+
+    def columns(row):
+        return slice(place[row] * win, (place[row] + 1) * win)
+
     def spread_rows(f, row_nos):
         for r in row_nos:
             for b, part in enumerate(shifts(adj[f, r].astype(F32))):
-                vs[f % 2, b * pad:(b + 1) * pad, r * win:(r + 1) * win] = part
+                vs[f % 2, b * pad:(b + 1) * pad, columns(r)] = part
 
     def first_conv(f, low, high):
-        columns = slice(low * win, high * win)
-        for side, w_ref in enumerate((w1_ref, w1_other)):
-            hs[f % 2, side, :, columns] = jnp.dot(
-                w_ref[:, 0:3 * pad], vs[f % 2, :, columns], preferred_element_type=F32)
+        part = slice(low * win, high * win)
+        both = w1_ref[...].reshape(6 * half, w1_ref.shape[2])
+        hs[f % 2, :, part] = jnp.dot(both[:, 0:3 * pad], vs[f % 2, :, part], preferred_element_type=F32)
 
     def begin(f):
         spread_rows(f, range(2, rows + 2))
-        first_conv(f, 2, rows + 2)
+        first_conv(f, 0, rows)
 
     def rim_conv(f):
         spread_rows(f, (0, 1, rims - 2, rims - 1))
-        first_conv(f, 0, 2)
-        first_conv(f, rims - 2, rims)
+        first_conv(f, rows, rims)
 
     def rest(f):
         for side in range(2):
             for p in range(hid_rows):
-                grad = sum(hs[f % 2, side, a * half:(a + 1) * half, (p + 2 - a) * win:(p + 3 - a) * win]
+                grad = sum(hs[f % 2, (3 * side + a) * half:(3 * side + a + 1) * half, columns(p + 2 - a)]
                            for a in range(3))
                 scaled = (slope_win[side, p].astype(F32) * grad).astype(BF16).astype(F32)
                 for b, part in enumerate(shifts(scaled)):
-                    ss[f % 2, side, b * half:(b + 1) * half, p * win:(p + 1) * win] = part
-        g = (jnp.dot(w2_ref[...], ss[f % 2, 0], preferred_element_type=F32)
-             + jnp.dot(w2_other[...], ss[f % 2, 1], preferred_element_type=F32))
-        return [adj[f, r + 2].astype(F32)
-                + sum(g[a * pad:(a + 1) * pad, (r + 2 - a) * win:(r + 3 - a) * win] for a in range(3))
-                for r in range(rows)]
+                    low = side * deep + b * half
+                    ss[f % 2, low:low + half, p * win:(p + 1) * win] = part
+        totals = [adj[f, r + 2].astype(F32) for r in range(rows)]
+        for p in range(0, hid_rows, 2):
+            offsets = [a for a in range(3) if p - 1 + a >= 0 and p - 2 + a < rows]
+            first, count = offsets[0], len(offsets)
+            g = jnp.dot(w2_ref[first * pad:(first + count) * pad, :], ss[f % 2, :, p * win:(p + 2) * win],
+                        preferred_element_type=F32)
+            for a in offsets:
+                for step in range(2):
+                    r = p + step - 2 + a
+                    if 0 <= r < rows:
+                        totals[r] = totals[r] + g[(a - first) * pad:(a - first + 1) * pad, step * win:(step + 1) * win]
+        return totals
 
     @pl.when(tm == 1)
     def _():
@@ -823,6 +840,7 @@
 
     layers = weight_in.shape[0]
     wide = round_up(3 * pad, 128)
+    deep = round_up(3 * half, 128)
 
     smem = pl.BlockSpec(memory_space=pltpu.SMEM)
     hbm = pl.BlockSpec(memory_space=pltpu.HBM)
@@ -846,13 +864,21 @@
             pltpu.VMEM((half * band, win), F32),
             pltpu.VMEM((band, half, win), BF16),
             pltpu.VMEM((2, hid_rows, half, win), BF16),
-            pltpu.VMEM((3 * half, wide), BF16),
-            pltpu.VMEM((3 * pad, 3 * half), BF16),
-            pltpu.VMEM((3 * half, wide), BF16),
-            pltpu.VMEM((3 * pad, 3 * half), BF16),
-            pltpu.VMEM((2, 3 * pad, rims * win), BF16),
-            pltpu.VMEM((2, 2, 3 * half, rims * win), F32),
-            pltpu.VMEM((2, 2, 3 * half, hid_rows * win), BF16),
+            *([
+                pltpu.VMEM((2, 3 * half, wide), BF16),
+                pltpu.VMEM((3 * pad, 2 * deep), BF16),
+                pltpu.VMEM((2, 3 * pad, rims * win), BF16),
+                pltpu.VMEM((2, 6 * half, rims * win), F32),
+                pltpu.VMEM((2, 2 * deep, hid_rows * win), BF16),
+            ] if pair else [
+                pltpu.VMEM((3 * half, wide), BF16),
+                pltpu.VMEM((3 * pad, 3 * half), BF16),
+                pltpu.VMEM((3 * half, wide), BF16),
+                pltpu.VMEM((3 * pad, 3 * half), BF16),
+                pltpu.VMEM((2, 3 * pad, rims * win), BF16),
+                pltpu.VMEM((2, 2, 3 * half, rims * win), F32),
+                pltpu.VMEM((2, 2, 3 * half, hid_rows * win), BF16),
+            ]),
             pltpu.SemaphoreType.DMA((fronts,)),
             pltpu.SemaphoreType.DMA((3,)),
             pltpu.SemaphoreType.DMA((2, fronts)),

time: 14.5 us -> 14.4 us (level)
  no operation moved by 1% of the time
where the time goes in v4:
time: 14.4 us; the launch traced here: 14.3 us
  Pallas kernels  13.4 us (93%)
  local copies, waits for them, and re-layouts  0.82 us (6%)
    pallas_call x1, Pallas kernels, per_device(): pl.pallas_call(functools.partial(pair_kernel if pair else chain_kernel, (...  13.4 us
    unnamed x1, local copies, waits for them, and re-layouts  0.82 us

profile of v4, /device:TPU:0, one launch (start us, length us, event | category | flops | bytes accessed | tf_op | source)
XLA Modules:
  0.0 14.3 jit_solution(16046645519606738703)
XLA Ops:
  0.0 13.4 %shard_map.64 = f32[1168,128]{1,0:T(8,128)S(1)} custom-call(s32[2]{0:T(128)} %layer_ref.1, s32[4]{0:T(128)} %bitcast.11, bf16[4,73,4,128]{3,2,1,0:T(4,128)(2,1)} %bitcast.9, bf16[512,128]{1,0:T(8,128)(2,1)} %bitcast.10, bf16[8,3,3,64,73]{4,3,2,1,0:T(8,128)(2,1)} %bitcast.8, bf16[8,3,3,64,73]{4,3,2,1,0:T(8,128)(2,1)} %w_out_hbm.1), custom_call_target="tpu_custom_call" | custom-call | tf_op jit(solution)/shard_map/pallas_call | solution.py:848
  13.4 0.8 %copy.9 = f32[4,1,73,4,128]{4,3,2,1,0:T(4,128)} copy(f32[4,1,73,4,128]{4,3,2,1,0:T(4,128)S(1)} %bitcast.7) | data formatting | bytes 1196032

commit v5 on v4

--- a/solution.py
+++ b/solution.py
@@ -18,7 +18,7 @@
 
 def pair_kernel(dims, layer_ref, mask_ref, inn_hbm, slopes_hbm, w_in_hbm, w_out_hbm, out_ref,
                 inn_ref, slopes_ref, w_in_ref, w_out_ref, w_wide, w_tall,
-                raw, frc, adj, res, slope_f32, slope_rows, slope_win, w1_ref, w2_ref, vs, hs, ss, load_inn, load_rest,
+                raw, frc, adj, packing, packed, folding, folded, slope_f32, slope_rows, slope_win, w1_ref, w2_ref, vs, hs, ss, load_inn, load_rest,
                 x_send, x_recv, r_send, r_recv, h_send, h_recv, w_send, w_recv, s_send, s_recv,
                 t_send, t_recv, above):
     fronts, chans, rows, win, half, band, lats, owners = dims
@@ -116,17 +116,33 @@
 
     starts = (core * 2, (1 - core) * 2)
 
+    def tail(n):
+        return round_up(chans * n + pad, 16)
+
+    def span(f):
+        low = tail(2 * f - 1) if f else 0
+        return pl.ds(low, tail(2 * f + 1) - low)
+
     def x_copy(k, f):
-        part = adj.at[f, pl.ds(2 + starts[k], 2)]
+        part = packed.at[k, span(f)]
         return pltpu.make_async_remote_copy(
             src_ref=part, dst_ref=part, send_sem=x_send.at[k, f], recv_sem=x_recv.at[k, f],
             device_id=opposite, device_id_type=MESH)
 
     def r_copy(k):
-        part = res.at[pl.ds(2 * k, 2)]
+        part = folded.at[span(k)]
         return pltpu.make_async_remote_copy(
             src_ref=part, dst_ref=part, send_sem=r_send.at[k], recv_sem=r_recv.at[k],
             device_id=opposite, device_id_type=MESH)
+
+    def unpacked(rows_of, n):
+        low = chans * n // 16 * 16
+        return rows_of[low:tail(n)].astype(F32)[chans * n - low:chans * n - low + pad]
+
+    def unpack(k, f):
+        x_copy(k, f).wait_recv()
+        for r in range(2):
+            adj[f, 2 + starts[k] + r] = unpacked(packed.at[k], 2 * f + r).astype(BF16)
 
     spans = ((3 - 3 * core, 5), (5 * core, 3))
 
@@ -283,28 +299,25 @@
     def columns(row):
         return slice(place[row] * win, (place[row] + 1) * win)
 
-    def spread_rows(f, row_nos):
-        for r in row_nos:
-            for b, part in enumerate(shifts(adj[f, r].astype(F32))):
-                vs[f % 2, b * pad:(b + 1) * pad, columns(r)] = part
-
-    def first_conv(f, low, high):
-        part = slice(low * win, high * win)
+    def convolve(own, rim):
+        slot = own % 2 if own is not None else (rim + 1) % 2
+        for f, row_nos in ((own, range(2, rows + 2)), (rim, (0, 1, rims - 2, rims - 1))):
+            for r in row_nos if f is not None else ():
+                for b, part in enumerate(shifts(adj[f, r].astype(F32))):
+                    vs[slot, b * pad:(b + 1) * pad, columns(r)] = part
+        low = 0 if own is not None else rows * win
+        high = (rims if rim is not None else rows) * win
         both = w1_ref[...].reshape(6 * half, w1_ref.shape[2])
-        hs[f % 2, :, part] = jnp.dot(both[:, 0:3 * pad], vs[f % 2, :, part], preferred_element_type=F32)
-
-    def begin(f):
-        spread_rows(f, range(2, rows + 2))
-        first_conv(f, 0, rows)
-
-    def rim_conv(f):
-        spread_rows(f, (0, 1, rims - 2, rims - 1))
-        first_conv(f, rows, rims)
+        product = jnp.dot(both[:, 0:3 * pad], vs[slot, :, low:high], preferred_element_type=F32)
+        if own is not None:
+            hs[own, :, 0:rows * win] = product[:, 0:rows * win]
+        if rim is not None:
+            hs[rim, :, rows * win:] = product[:, rows * win - low:]
 
     def rest(f):
         for side in range(2):
             for p in range(hid_rows):
-                grad = sum(hs[f % 2, (3 * side + a) * half:(3 * side + a + 1) * half, columns(p + 2 - a)]
+                grad = sum(hs[f, (3 * side + a) * half:(3 * side + a + 1) * half, columns(p + 2 - a)]
                            for a in range(3))
                 scaled = (slope_win[side, p].astype(F32) * grad).astype(BF16).astype(F32)
                 for b, part in enumerate(shifts(scaled)):
@@ -331,17 +344,19 @@
             load.start()
         clear_rims()
         if pad > chans:
-            for f in range(fronts):
-                for r in range(rows):
-                    adj[f, r + 2, chans:pad, :] = jnp.zeros((pad - chans, win), BF16)
-
-        def take(f):
+            for r in range(rows):
+                adj[far, r + 2, chans:pad, :] = jnp.zeros((pad - chans, win), BF16)
+
+        filled = 2 * far * chans
+        packing[:, filled:, :] = jnp.zeros((2, tail(2 * far - 1) - filled, win), F32)
+        folding[4 * chans:, :] = jnp.zeros((tail(3) - 4 * chans, win), F32)
+        for f in range(far):
             inn_copy(f).wait()
             load_raw(f)
             for r in range(rows):
-                adj[f, r + 2, 0:chans, :] = forcing_row(r).astype(BF16)
-
-        take(0)
+                kind = core if r < 2 else 1 - core
+                packing[kind, chans * (2 * f + r % 2):chans * (2 * f + r % 2 + 1), :] = forcing_row(r)
+        packed[...] = packing[...].astype(BF16)
         enter()
         x_copy(0, 0).start()
 
@@ -350,11 +365,13 @@
             x_copy(0, 0).wait_send()
 
         for f in range(1, far):
-            take(f)
             x_copy(0, f).start()
         for f in range(far):
             x_copy(1, f).start()
-        take(far)
+        inn_copy(far).wait()
+        load_raw(far)
+        for r in range(rows):
+            adj[far, r + 2, 0:chans, :] = forcing_row(r).astype(BF16)
 
         @pl.when(not_first)
         def _():
@@ -373,24 +390,32 @@
         def _():
             halo_up(far).start()
 
-        for f in range(fronts):
+        for f in reversed(range(fronts)):
+            if f < far:
+                load_raw(f)
             for r in range(rows):
-                put_out(f, r, adj[f, r + 2, 0:chans, :].astype(F32))
+                put_out(f, r, forcing_row(r))
 
         w1_copy.wait_recv()
-        begin(far)
+        convolve(far, None)
         t_copy(0).wait_recv()
         s_copy.start()
         halos_here(far)
-        rim_conv(far)
+        convolve(None, far)
         w2_copy.wait_recv()
         t_copy(1).wait_recv()
         own_slopes()
         slopes_here()
         for r, value in enumerate(rest(far)):
-            res[r] = value.astype(BF16)
-            if r % 2 == 1:
-                r_copy(r // 2).start()
+            folding[chans * r:chans * (r + 1), :] = value[0:chans]
+        folded[...] = folding[...].astype(BF16)
+        r_copy(0).start()
+
+        @pl.when(core == 1)
+        def _():
+            r_copy(0).wait_send()
+
+        r_copy(1).start()
 
         all_sent()
         halos_sent(far)
@@ -401,8 +426,12 @@
         for k in range(2):
             for f in range(1 - k, far):
                 x_copy(k, f).wait_send()
-        for k in range(2):
-            r_copy(k).wait_send()
+
+        @pl.when(core == 0)
+        def _():
+            r_copy(0).wait_send()
+
+        r_copy(1).wait_send()
 
     @pl.when(tm == 0)
     def _():
@@ -418,12 +447,21 @@
             slope_rows[r] = slope_f32[pl.ds(r, half, stride=band), :].astype(BF16)
         enter()
         slope_down(start, 1)
-        for k in range(2):
-            t_copy(k).start()
+        t_copy(0).start()
+
+        @pl.when(core == 0)
+        def _():
+            t_copy(1).start()
+
         slope_down(start, 0)
         s_copy.start()
         own_slopes()
         prepare_weights()
+
+        @pl.when(core == 1)
+        def _():
+            t_copy(1).start()
+
         wait_above()
         slope_up(start, 1)
         slope_up(start, 0)
@@ -437,31 +475,49 @@
                 frc[f, r, 0:chans, :] = forcing_row(r).astype(BF16)
 
         for f in range(far):
-            x_copy(0, f).wait_recv()
+            unpack(0, f)
             pass_on(0, f)
 
         w1_copy.wait_recv()
         w2_copy.wait_recv()
         slopes_here()
 
-        def finish(f):
+        def finish(f, following):
             halos_here(f)
-            rim_conv(f)
+            convolve(following, f)
             for r, value in enumerate(rest(f)):
                 put_out(f, r, value[0:chans] + frc[f, r, 0:chans, :].astype(F32))
 
-        for f in range(far):
-            x_copy(1, f).wait_recv()
+        def inner_rows(f):
+            unpack(1, f)
             pass_on(1, f)
-            if f > 0:
-                finish(f - 1)
-            begin(f)
-        finish(far - 1)
+
+        @pl.when(core == 0)
+        def _():
+            for f in range(far):
+                inner_rows(f)
+                if f < far - 1 or far < 3:
+                    convolve(f, None)
+                if f < far - 2:
+                    finish(f, None)
+            for f in range(max(far - 2, 0), far):
+                finish(f, far - 1 if far > 2 and f == far - 2 else None)
+
+        @pl.when(core == 1)
+        def _():
+            for f in range(far):
+                inner_rows(f)
+                if f < far - 1:
+                    convolve(f, None)
+            for f in range(far):
+                if far == 1:
+                    convolve(f, None)
+                finish(f, far - 1 if far > 1 and f == 0 else None)
 
         for k in range(2):
             r_copy(k).wait_recv()
             for r in (2 * k, 2 * k + 1):
-                put_out(far, r, res[r, 0:chans, :].astype(F32) + frc[far, r, 0:chans, :].astype(F32))
+                put_out(far, r, unpacked(folded, r)[0:chans] + frc[far, r, 0:chans, :].astype(F32))
 
         all_sent()
         for f in range(far):
@@ -839,6 +895,8 @@
     rims, hid_rows = rows + 4, rows + 2
 
     layers = weight_in.shape[0]
+    packed_rows = round_up(chans * (2 * fronts - 3) + pad, 16)
+    folded_rows = round_up(3 * chans + pad, 16)
     wide = round_up(3 * pad, 128)
     deep = round_up(3 * half, 128)
 
@@ -860,7 +918,12 @@
             pltpu.VMEM((chans * rows, win), F32),
             pltpu.VMEM((fronts, rows, pad, win), BF16),
             pltpu.VMEM((fronts, rims, pad, win), BF16),
-            *([pltpu.VMEM((rows, pad, win), BF16)] if pair else []),
+            *([
+                pltpu.VMEM((2, packed_rows, win), F32),
+                pltpu.VMEM((2, packed_rows, win), BF16),
+                pltpu.VMEM((folded_rows, win), F32),
+                pltpu.VMEM((folded_rows, win), BF16),
+            ] if pair else []),
             pltpu.VMEM((half * band, win), F32),
             pltpu.VMEM((band, half, win), BF16),
             pltpu.VMEM((2, hid_rows, half, win), BF16),
@@ -868,7 +931,7 @@
                 pltpu.VMEM((2, 3 * half, wide), BF16),
                 pltpu.VMEM((3 * pad, 2 * deep), BF16),
                 pltpu.VMEM((2, 3 * pad, rims * win), BF16),
-                pltpu.VMEM((2, 6 * half, rims * win), F32),
+                pltpu.VMEM((fronts, 6 * half, rims * win), F32),
                 pltpu.VMEM((2, 2 * deep, hid_rows * win), BF16),
             ] if pair else [
                 pltpu.VMEM((3 * half, wide), BF16),

time: 14.4 us -> 14.4 us (level)
  the two profiles are of different devices: /device:TPU:0 before, /device:TPU:1 now
where the time goes in v5:
time: 14.4 us; the launch traced here: 14.2 us
  Pallas kernels  13.4 us (93%)
  local copies, waits for them, and re-layouts  0.82 us (6%)
    pallas_call x1, Pallas kernels, per_device(): pl.pallas_call(functools.partial(pair_kernel if pair else chain_kernel, (...  13.4 us
    unnamed x1, local copies, waits for them, and re-layouts  0.82 us

profile of v5, /device:TPU:1, one launch (start us, length us, event | category | flops | bytes accessed | tf_op | source)
XLA Modules:
  0.0 14.2 jit_solution(18215930641443270850)
XLA Ops:
  0.0 13.4 %shard_map.64 = f32[1168,128]{1,0:T(8,128)S(1)} custom-call(s32[2]{0:T(128)} %layer_ref.1, s32[4]{0:T(128)} %bitcast.11, bf16[4,73,4,128]{3,2,1,0:T(4,128)(2,1)} %bitcast.9, bf16[512,128]{1,0:T(8,128)(2,1)} %bitcast.10, bf16[8,3,3,64,73]{4,3,2,1,0:T(8,128)(2,1)} %bitcast.8, bf16[8,3,3,64,73]{4,3,2,1,0:T(8,128)(2,1)} %w_out_hbm.1), custom_call_target="tpu_custom_call" | custom-call | tf_op jit(solution)/shard_map/pallas_call | solution.py:906
  13.4 0.8 %copy.9 = f32[4,1,73,4,128]{4,3,2,1,0:T(4,128)} copy(f32[4,1,73,4,128]{4,3,2,1,0:T(4,128)S(1)} %bitcast.7) | data formatting | bytes 1196032

commit v6 on v4

--- a/solution.py
+++ b/solution.py
@@ -389,8 +389,13 @@
         slopes_here()
         for r, value in enumerate(rest(far)):
             res[r] = value.astype(BF16)
-            if r % 2 == 1:
-                r_copy(r // 2).start()
+        r_copy(0).start()
+
+        @pl.when(core == 1)
+        def _():
+            r_copy(0).wait_send()
+
+        r_copy(1).start()
 
         all_sent()
         halos_sent(far)
@@ -401,8 +406,12 @@
         for k in range(2):
             for f in range(1 - k, far):
                 x_copy(k, f).wait_send()
-        for k in range(2):
-            r_copy(k).wait_send()
+
+        @pl.when(core == 0)
+        def _():
+            r_copy(0).wait_send()
+
+        r_copy(1).wait_send()
 
     @pl.when(tm == 0)
     def _():
@@ -418,12 +427,21 @@
             slope_rows[r] = slope_f32[pl.ds(r, half, stride=band), :].astype(BF16)
         enter()
         slope_down(start, 1)
-        for k in range(2):
-            t_copy(k).start()
+        t_copy(0).start()
+
+        @pl.when(core == 0)
+        def _():
+            t_copy(1).start()
+
         slope_down(start, 0)
         s_copy.start()
         own_slopes()
         prepare_weights()
+
+        @pl.when(core == 1)
+        def _():
+            t_copy(1).start()
+
         wait_above()
         slope_up(start, 1)
         slope_up(start, 0)

time: 14.4 us -> 14.4 us (level)
  no operation moved by 1% of the time
where the time goes in v6:
time: 14.4 us; the launch traced here: 14.2 us
  Pallas kernels  13.4 us (93%)
  local copies, waits for them, and re-layouts  0.82 us (6%)
    pallas_call x1, Pallas kernels, per_device(): pl.pallas_call(functools.partial(pair_kernel if pair else chain_kernel, (...  13.4 us
    unnamed x1, local copies, waits for them, and re-layouts  0.82 us

profile of v6, /device:TPU:0, one launch (start us, length us, event | category | flops | bytes accessed | tf_op | source)
XLA Modules:
  0.0 14.2 jit_solution(10915455855698138505)
XLA Ops:
  0.0 13.4 %shard_map.64 = f32[1168,128]{1,0:T(8,128)S(1)} custom-call(s32[2]{0:T(128)} %layer_ref.1, s32[4]{0:T(128)} %bitcast.11, bf16[4,73,4,128]{3,2,1,0:T(4,128)(2,1)} %bitcast.9, bf16[512,128]{1,0:T(8,128)(2,1)} %bitcast.10, bf16[8,3,3,64,73]{4,3,2,1,0:T(8,128)(2,1)} %bitcast.8, bf16[8,3,3,64,73]{4,3,2,1,0:T(8,128)(2,1)} %w_out_hbm.1), custom_call_target="tpu_custom_call" | custom-call | tf_op jit(solution)/shard_map/pallas_call | solution.py:866
  13.4 0.8 %copy.9 = f32[4,1,73,4,128]{4,3,2,1,0:T(4,128)} copy(f32[4,1,73,4,128]{4,3,2,1,0:T(4,128)S(1)} %bitcast.7) | data formatting | bytes 1196032

commit v7 on v6

--- a/solution.py
+++ b/solution.py
@@ -283,23 +283,20 @@
     def columns(row):
         return slice(place[row] * win, (place[row] + 1) * win)
 
-    def spread_rows(f, row_nos):
-        for r in row_nos:
-            for b, part in enumerate(shifts(adj[f, r].astype(F32))):
-                vs[f % 2, b * pad:(b + 1) * pad, columns(r)] = part
-
-    def first_conv(f, low, high):
-        part = slice(low * win, high * win)
+    def convolve(own, rim):
+        slot = own % 2 if own is not None else (rim + 1) % 2
+        for f, row_nos in ((own, range(2, rows + 2)), (rim, (0, 1, rims - 2, rims - 1))):
+            for r in row_nos if f is not None else ():
+                for b, part in enumerate(shifts(adj[f, r].astype(F32))):
+                    vs[slot, b * pad:(b + 1) * pad, columns(r)] = part
+        low = 0 if own is not None else rows * win
+        high = (rims if rim is not None else rows) * win
         both = w1_ref[...].reshape(6 * half, w1_ref.shape[2])
-        hs[f % 2, :, part] = jnp.dot(both[:, 0:3 * pad], vs[f % 2, :, part], preferred_element_type=F32)
-
-    def begin(f):
-        spread_rows(f, range(2, rows + 2))
-        first_conv(f, 0, rows)
-
-    def rim_conv(f):
-        spread_rows(f, (0, 1, rims - 2, rims - 1))
-        first_conv(f, rows, rims)
+        product = jnp.dot(both[:, 0:3 * pad], vs[slot, :, low:high], preferred_element_type=F32)
+        if own is not None:
+            hs[own % 2, :, 0:rows * win] = product[:, 0:rows * win]
+        if rim is not None:
+            hs[rim % 2, :, rows * win:] = product[:, rows * win - low:]
 
     def rest(f):
         for side in range(2):
@@ -378,11 +375,11 @@
                 put_out(f, r, adj[f, r + 2, 0:chans, :].astype(F32))
 
         w1_copy.wait_recv()
-        begin(far)
+        convolve(far, None)
         t_copy(0).wait_recv()
         s_copy.start()
         halos_here(far)
-        rim_conv(far)
+        convolve(None, far)
         w2_copy.wait_recv()
         t_copy(1).wait_recv()
         own_slopes()
@@ -462,9 +459,9 @@
         w2_copy.wait_recv()
         slopes_here()
 
-        def finish(f):
+        def finish(f, following):
             halos_here(f)
-            rim_conv(f)
+            convolve(following, f)
             for r, value in enumerate(rest(f)):
                 put_out(f, r, value[0:chans] + frc[f, r, 0:chans, :].astype(F32))
 
@@ -472,9 +469,10 @@
             x_copy(1, f).wait_recv()
             pass_on(1, f)
             if f > 0:
-                finish(f - 1)
-            begin(f)
-        finish(far - 1)
+                finish(f - 1, f)
+            else:
+                convolve(f, None)
+        finish(far - 1, None)
 
         for k in range(2):
             r_copy(k).wait_recv()

time: 14.4 us -> 14.4 us (level)
  no operation moved by 1% of the time
where the time goes in v7:
time: 14.4 us; the launch traced here: 14.3 us
  Pallas kernels  13.4 us (93%)
  local copies, waits for them, and re-layouts  0.82 us (6%)
    pallas_call x1, Pallas kernels, per_device(): pl.pallas_call(functools.partial(pair_kernel if pair else chain_kernel, (...  13.4 us
    unnamed x1, local copies, waits for them, and re-layouts  0.82 us

profile of v7, /device:TPU:0, one launch (start us, length us, event | category | flops | bytes accessed | tf_op | source)
XLA Modules:
  0.0 14.3 jit_solution(1834250698175369484)
XLA Ops:
  0.0 13.4 %shard_map.64 = f32[1168,128]{1,0:T(8,128)S(1)} custom-call(s32[2]{0:T(128)} %layer_ref.1, s32[4]{0:T(128)} %bitcast.11, bf16[4,73,4,128]{3,2,1,0:T(4,128)(2,1)} %bitcast.9, bf16[512,128]{1,0:T(8,128)(2,1)} %bitcast.10, bf16[8,3,3,64,73]{4,3,2,1,0:T(8,128)(2,1)} %bitcast.8, bf16[8,3,3,64,73]{4,3,2,1,0:T(8,128)(2,1)} %w_out_hbm.1), custom_call_target="tpu_custom_call" | custom-call | tf_op jit(solution)/shard_map/pallas_call | solution.py:864
  13.4 0.8 %copy.9 = f32[4,1,73,4,128]{4,3,2,1,0:T(4,128)} copy(f32[4,1,73,4,128]{4,3,2,1,0:T(4,128)S(1)} %bitcast.7) | data formatting | bytes 1196032
